TPU v7x, 32 devices: a whole 2x2x4 slice. The times are simulated.
32 devices in a mesh: group: 2 (over x), owner: 16 (over z, y, core).
Axes of the slice: x: 2, y: 2, z: 4, core: 2. Of those that a mesh axis runs over, the one named last changes fastest.
Arguments:
- tokens: bfloat16 [4096, 2048], P(('group', 'owner')), parts along dimension 0, may hold values from -6 to 6
- cotangent: bfloat16 [4096, 2048], P(('group', 'owner')), parts along dimension 0, may hold values from -6 to 6
- route_ids: int32 [4096, 3], P('group'), parts along dimension 0, may hold values from 0 to 15, as said below
- gate_probs: float32 [4096, 3], P(('group', 'owner')), parts along dimension 0, may hold values from 0.05 to 1
- w_gate: bfloat16 [16, 2048, 384], P('owner'), may hold values from -0.125 to 0.125
- w_up: bfloat16 [16, 2048, 384], P('owner'), may hold values from -0.125 to 0.125
- w_down: bfloat16 [16, 384, 2048], P('owner'), may hold values from -0.3125 to 0.3125
Outputs:
- expert_out: bfloat16 [4096, 2048], P(('group', 'owner')), parts along dimension 0
- grad_tokens: bfloat16 [4096, 2048], P(('group', 'owner')), parts along dimension 0
- grad_gates: float32 [4096, 3], P(('group', 'owner')), parts along dimension 0
- grad_w_gate: bfloat16 [32, 2048, 384], P(('group', 'owner')), parts along dimension 0
- grad_w_up: bfloat16 [32, 2048, 384], P(('group', 'owner')), parts along dimension 0
- grad_w_down: bfloat16 [32, 384, 2048], P(('group', 'owner')), parts along dimension 0
There are 2 independent parts, one for each index of `group`. A program takes and returns all parts, laid end to end along the dimension named above; an argument that names none is the same for every part. Nothing has to cross between parts.
Inputs may be any that keep to these rules, and one draw needn't show every extreme that they name: `route_ids`: each token names 3 different experts. The 128 tokens of one owner device (aligned blocks) name any one expert at most 48 times, and some expert exactly 48 times.
All inputs are finite; a program needn't handle non-finite values.
Results may differ from a plain program's by a relative error of at most 0.008.
Values may be sent and summed in bfloat16 or wider, within the bound.
A program may use at most 128 MiB of HBM per device.

v0:
```python
import functools

import jax
import jax.numpy as jnp
from jax import lax
from jax.experimental import pallas as pl
from jax.experimental.pallas import tpu as pltpu
from jax.sharding import PartitionSpec as P


def expert_pass(tokens_in, cotan_in, gate_w, up_w, down_w):
    gate_pre = jnp.dot(tokens_in, gate_w, preferred_element_type=jnp.float32)
    up_pre = jnp.dot(tokens_in, up_w, preferred_element_type=jnp.float32)
    gate_sig = jax.nn.sigmoid(gate_pre)
    gate_act = gate_pre * gate_sig
    hidden = (gate_act * up_pre).astype(jnp.bfloat16)
    expert_y = jnp.dot(hidden, down_w, preferred_element_type=jnp.float32).astype(jnp.bfloat16)
    d_hidden = jnp.dot(cotan_in, down_w.T, preferred_element_type=jnp.float32)
    grad_gate_pre = (d_hidden * up_pre * gate_sig * (1.0 + gate_pre * (1.0 - gate_sig))).astype(
        jnp.bfloat16
    )
    grad_up_pre = (d_hidden * gate_act).astype(jnp.bfloat16)
    expert_dx = (
        jnp.dot(grad_gate_pre, gate_w.T, preferred_element_type=jnp.float32)
        + jnp.dot(grad_up_pre, up_w.T, preferred_element_type=jnp.float32)
    ).astype(jnp.bfloat16)
    return (expert_y, expert_dx, hidden, grad_gate_pre, grad_up_pre)


def local(tokens, cotangent, route_ids, gate_probs, w_gate, w_up, w_down):
    owner_count = lax.axis_size("owner")
    my_index = lax.axis_index("owner")
    token_rows, model_width = tokens.shape
    route_count = route_ids.shape[1]
    slot_depth = 2 * token_rows * route_count // owner_count
    assign_count = token_rows * route_count
    slot_total = owner_count * slot_depth
    expert_ids = jnp.arange(owner_count, dtype=jnp.int32)
    id_table = route_ids.reshape(owner_count, assign_count)
    my_routes = lax.dynamic_index_in_dim(id_table, my_index, 0, keepdims=False)
    one_hot = (my_routes[:, None] == expert_ids[None, :]).astype(jnp.int32)
    rank_within = jnp.sum((jnp.cumsum(one_hot, axis=0) - one_hot) * one_hot, axis=1)
    source_loads = jnp.sum((id_table == my_index).astype(jnp.int32), axis=1)
    scaled_cot = (gate_probs[:, :, None] * cotangent[:, None, :].astype(jnp.float32)).astype(
        jnp.bfloat16
    )
    token_copies = jnp.broadcast_to(tokens[:, None, :], (token_rows, route_count, model_width))
    zero_row = jnp.zeros((1, model_width), jnp.bfloat16)
    token_ext = jnp.concatenate([token_copies.reshape(assign_count, model_width), zero_row], axis=0)
    cotan_ext = jnp.concatenate([scaled_cot.reshape(assign_count, model_width), zero_row], axis=0)
    is_hot = jnp.zeros((assign_count,), dtype=bool)
    slot_target = jnp.where(is_hot, slot_total, my_routes * slot_depth + rank_within)
    slot_source = jnp.full((slot_total + 1,), assign_count, jnp.int32)
    slot_source = slot_source.at[slot_target].set(jnp.arange(assign_count, dtype=jnp.int32))[
        :slot_total
    ]
    send_tokens = token_ext[slot_source].reshape(owner_count, slot_depth, model_width)
    send_cotan = cotan_ext[slot_source].reshape(owner_count, slot_depth, model_width)
    got_tokens, got_cotan = (
        lax.all_to_all(send_tokens, "owner", split_axis=0, concat_axis=0, tiled=True),
        lax.all_to_all(send_cotan, "owner", split_axis=0, concat_axis=0, tiled=True),
    )
    live_slot = (jnp.arange(slot_depth, dtype=jnp.int32)[None, :] < source_loads[:, None]).reshape(
        slot_total
    )
    compact_pos = jnp.cumsum(live_slot.astype(jnp.int32)) - 1
    live_total = jnp.sum(source_loads)
    compact_from = jnp.full((slot_total,), slot_total, jnp.int32)
    compact_from = compact_from.at[jnp.where(live_slot, compact_pos, slot_total)].set(
        jnp.arange(slot_total, dtype=jnp.int32), mode="drop"
    )
    flat_tokens = jnp.concatenate([got_tokens.reshape(slot_total, model_width), zero_row], axis=0)
    flat_cotan = jnp.concatenate([got_cotan.reshape(slot_total, model_width), zero_row], axis=0)
    compact_tokens = flat_tokens[compact_from]
    compact_cotan = flat_cotan[compact_from]
    gate_w = w_gate[0]
    up_w = w_up[0]
    down_w = w_down[0]
    hidden_width = gate_w.shape[1]

    def block_step(turn_index, carried):
        out_rows, back_rows, grad_gate, grad_up, grad_down = carried
        row_start = turn_index * assign_count
        block_tokens = lax.dynamic_slice_in_dim(compact_tokens, row_start, assign_count, 0)
        block_cotan = lax.dynamic_slice_in_dim(compact_cotan, row_start, assign_count, 0)
        expert_y, expert_dx, hidden, grad_gate_pre, grad_up_pre = expert_pass(
            block_tokens, block_cotan, gate_w, up_w, down_w
        )
        out_rows = lax.dynamic_update_slice_in_dim(out_rows, expert_y, row_start, 0)
        back_rows = lax.dynamic_update_slice_in_dim(back_rows, expert_dx, row_start, 0)
        grad_gate = grad_gate + jnp.dot(
            block_tokens.T, grad_gate_pre, preferred_element_type=jnp.float32
        )
        grad_up = grad_up + jnp.dot(block_tokens.T, grad_up_pre, preferred_element_type=jnp.float32)
        grad_down = grad_down + jnp.dot(hidden.T, block_cotan, preferred_element_type=jnp.float32)
        return (out_rows, back_rows, grad_gate, grad_up, grad_down)

    turn_count = (live_total + assign_count - 1) // assign_count
    initial = (
        jnp.zeros((slot_total, model_width), jnp.bfloat16),
        jnp.zeros((slot_total, model_width), jnp.bfloat16),
        jnp.zeros((model_width, hidden_width), jnp.float32),
        jnp.zeros((model_width, hidden_width), jnp.float32),
        jnp.zeros((hidden_width, model_width), jnp.float32),
    )
    out_rows, back_rows, grad_gate, grad_up, grad_down = lax.fori_loop(
        0, turn_count, block_step, initial
    )
    return_pos = jnp.where(live_slot, compact_pos, 0)
    return_y = out_rows[return_pos].reshape(owner_count, slot_depth, model_width)
    return_dx = back_rows[return_pos].reshape(owner_count, slot_depth, model_width)
    came_y, came_dx = (
        lax.all_to_all(return_y, "owner", split_axis=0, concat_axis=0, tiled=True),
        lax.all_to_all(return_dx, "owner", split_axis=0, concat_axis=0, tiled=True),
    )
    pick_slot = jnp.where(is_hot, 0, slot_target)
    routed_rows = came_y.reshape(slot_total, model_width)[pick_slot]
    routed_backs = came_dx.reshape(slot_total, model_width)[pick_slot]
    grad_gate_out = grad_gate.astype(jnp.bfloat16)
    grad_up_out = grad_up.astype(jnp.bfloat16)
    grad_down_out = grad_down.astype(jnp.bfloat16)
    routed_y = routed_rows.reshape(token_rows, route_count, model_width).astype(jnp.float32)
    expert_out = jnp.sum(gate_probs[:, :, None] * routed_y, axis=1).astype(jnp.bfloat16)
    grad_tokens = jnp.sum(
        routed_backs.reshape(token_rows, route_count, model_width).astype(jnp.float32), axis=1
    ).astype(jnp.bfloat16)
    grad_gates = jnp.sum(routed_y * cotangent[:, None, :].astype(jnp.float32), axis=2)
    return (
        expert_out,
        grad_tokens,
        grad_gates,
        grad_gate_out[None],
        grad_up_out[None],
        grad_down_out[None],
    )


def ring_width(mesh):
    coords = [getattr(d, "coords", None) for d in mesh.devices.reshape(mesh.devices.shape[0], -1)[0]]
    if any(c is None for c in coords):
        return 2
    return 2 if len({c[1] for c in coords}) == 2 else 1


def ring_kernel(
    y_size, owners, cap,
    route_ref, prob_ref, tok_ref, cot_ref, wg_hbm, wu_hbm, wd_hbm,
    eo_ref, gt_ref, gg_ref, og_ref, ou_ref, od_ref,
    slots, probs, sib, sib_t, ring, ring_t, gates, sel_buf, rows, cot_rows, prow, back,
    hid, gpre, upre, wg_ref, wu_ref, wd_ref,
    ag_send, ag_recv, agt_send, agt_recv, sf_send, sf_recv, sft_send, sft_recv,
    sp_send, sp_recv, spt_send, spt_recv, rs_send, rs_recv, rst_send, rst_recv, loc,
):
    f32, bf16 = jnp.float32, jnp.bfloat16
    chips = owners // 2
    half = chips // 2
    depth = chips // y_size
    tok, width = tok_ref.shape
    me = lax.axis_index("owner")
    chip = me // 2
    core = me % 2
    if y_size == 2:
        cz, cy = chip // 2, chip % 2
        pos = (1 - cy) * cz + cy * (2 * depth - 1 - cz)
    else:
        pos = chip

    def owner_at(offset, core_index):
        p = (pos + offset + chips) % chips
        if y_size == 2:
            py = p // depth
            pz = (1 - py) * p + py * (2 * depth - 1 - p)
            return (pz * 2 + py) * 2 + core_index
        return p * 2 + core_index

    right, left, twin = owner_at(1, core), owner_at(-1, core), owner_at(0, 1 - core)

    loads = [
        pltpu.make_async_copy(tok_ref, slots.at[0, :, pl.ds(0, width)], loc.at[0]),
        pltpu.make_async_copy(cot_ref, slots.at[0, :, pl.ds(width, width)], loc.at[1]),
        pltpu.make_async_copy(prob_ref, probs.at[0], loc.at[2]),
        pltpu.make_async_copy(wg_hbm, wg_ref, loc.at[3]),
        pltpu.make_async_copy(wu_hbm, wu_ref, loc.at[4]),
        pltpu.make_async_copy(wd_hbm, wd_ref, loc.at[5]),
    ]
    for c in loads:
        c.start()
    barrier = pltpu.get_barrier_semaphore()
    for other in (right, left, twin):
        pl.semaphore_signal(
            barrier, inc=1, device_id={"owner": other}, device_id_type=pl.DeviceIdType.MESH
        )
    pl.semaphore_wait(barrier, 3)
    for c in loads[:3]:
        c.wait()

    def remote(src, dst, send, recv, to):
        return pltpu.make_async_remote_copy(
            src_ref=src, dst_ref=dst, send_sem=send, recv_sem=recv,
            device_id={"owner": to}, device_id_type=pl.DeviceIdType.MESH,
        )

    lo, hi = pl.ds(0, width), pl.ds(width, width)

    def gather_copies(s):
        a, b = (-(s - 1)) % chips, s - 1
        c, d = (-s) % chips, s
        i = s - 1
        if s < half:
            return [
                remote(slots.at[a], slots.at[c], ag_send.at[0, i], ag_recv.at[0, i], right),
                remote(slots.at[b], slots.at[d], ag_send.at[1, i], ag_recv.at[1, i], left),
                remote(probs.at[a], probs.at[c], agt_send.at[0, i], agt_recv.at[0, i], right),
                remote(probs.at[b], probs.at[d], agt_send.at[1, i], agt_recv.at[1, i], left),
            ]
        return [
            remote(slots.at[a, :, lo], slots.at[half, :, lo], ag_send.at[0, i], ag_recv.at[0, i], right),
            remote(slots.at[b, :, hi], slots.at[half, :, hi], ag_send.at[1, i], ag_recv.at[1, i], left),
            remote(probs.at[a], probs.at[half], agt_send.at[0, i], agt_recv.at[0, i], right),
        ]

    def twin_copies(o):
        return [
            remote(slots.at[o], slots.at[chips + o], sf_send.at[o], sf_recv.at[o], twin),
            remote(probs.at[o], probs.at[chips + o], sft_send.at[o], sft_recv.at[o], twin),
        ]

    def partial_copies(o):
        return [
            remote(slots.at[chips + o], sib.at[o], sp_send.at[o], sp_recv.at[o], twin),
            remote(gates.at[chips + o], sib_t.at[o], spt_send.at[o], spt_recv.at[o], twin),
        ]

    def offsets(d):
        return [d] if d in (0, half) else [(-d) % chips, d]

    first_row = [0] * (half + 1)
    for d in range(half):
        first_row[d + 1] = first_row[d] + 2 * cap * len(offsets(d))
    chunk = 512 if width % 512 == 0 else 128
    contract0 = (((0,), (0,)), ((), ()))
    contract1 = (((1,), (1,)), ((), ()))

    def cols(i, base=0):
        return pl.ds(pl.multiple_of(base + i * chunk, 128), chunk)

    def over_chunks(body, init=0):
        return lax.fori_loop(0, width // chunk, body, init)

    upper = (
        lax.broadcasted_iota(jnp.int32, (tok, tok), 0)
        <= lax.broadcasted_iota(jnp.int32, (tok, tok), 1)
    ).astype(bf16)

    def batch_slots(d):
        return [(o, core) for o in offsets(d)] + [(chips + o, 1 - core) for o in offsets(d)]

    def compute(d):
        r0 = first_row[d]
        entries = batch_slots(d)
        m = cap * len(entries)
        marks = []
        for i, (j, source_core) in enumerate(entries):
            owner = owner_at(j % chips, source_core)
            mark = (route_ref[owner] == me).astype(f32)
            hit = jnp.sum(mark, axis=0, keepdims=True)
            count = jnp.dot(
                jnp.broadcast_to(hit, (8, tok)).astype(bf16), upper, preferred_element_type=f32
            )[0:1]
            rank = jnp.where(hit > 0, count - 1, -1.0)
            sel = lax.broadcasted_iota(jnp.int32, (cap, tok), 0).astype(f32) == rank
            weight = jnp.sum(probs[j] * mark, axis=0, keepdims=True)
            prow[i * cap : (i + 1) * cap, :] = jnp.sum(
                jnp.where(sel, weight, 0.0), axis=1, keepdims=True
            )
            sel_buf[j] = sel.astype(bf16)
            marks.append((mark, sel))

            def pick(k, carry, i=i, j=j):
                s = sel_buf[j]
                rows[r0 + i * cap : r0 + (i + 1) * cap, cols(k)] = jnp.dot(
                    s, slots[j, :, cols(k)], preferred_element_type=f32
                ).astype(bf16)
                c = jnp.dot(s, slots[j, :, cols(k, width)], preferred_element_type=f32)
                cot_rows[i * cap : (i + 1) * cap, cols(k)] = c.astype(bf16)
                rows[r0 + i * cap : r0 + (i + 1) * cap, cols(k, width)] = (
                    c * prow[i * cap : (i + 1) * cap, :]
                ).astype(bf16)
                return carry

            over_chunks(pick)
        x = rows[r0 : r0 + m, 0:width]
        gate_pre = jnp.dot(x, wg_ref[...], preferred_element_type=f32)
        up_pre = jnp.dot(x, wu_ref[...], preferred_element_type=f32)
        sig = jax.nn.sigmoid(gate_pre)
        act = gate_pre * sig
        hid[r0 : r0 + m, :] = (act * up_pre).astype(bf16)
        d_hidden = lax.dot_general(
            rows[r0 : r0 + m, width : 2 * width], wd_ref[...], contract1,
            preferred_element_type=f32,
        )
        gpre[r0 : r0 + m, :] = (
            d_hidden * up_pre * sig * (1.0 + gate_pre * (1.0 - sig))
        ).astype(bf16)
        upre[r0 : r0 + m, :] = (d_hidden * act).astype(bf16)

        def produce(k, total):
            y = jnp.dot(
                hid[r0 : r0 + m, :], wd_ref[:, cols(k)], preferred_element_type=f32
            ).astype(bf16).astype(f32)
            back[0:m, cols(k)] = (y * prow[0:m, :]).astype(bf16)
            dx = lax.dot_general(
                gpre[r0 : r0 + m, :], wg_ref[cols(k), :], contract1, preferred_element_type=f32
            ) + lax.dot_general(
                upre[r0 : r0 + m, :], wu_ref[cols(k), :], contract1, preferred_element_type=f32
            )
            back[0:m, cols(k, width)] = dx.astype(bf16)
            return total + jnp.sum(
                y * cot_rows[0:m, cols(k)].astype(f32), axis=1, keepdims=True
            )

        dots = over_chunks(produce, jnp.zeros((m, 1), f32))
        for i, (j, _) in enumerate(entries):
            mark, sel = marks[i]
            lane = jnp.sum(
                jnp.where(sel, dots[i * cap : (i + 1) * cap], 0.0), axis=0, keepdims=True
            )
            gates[j] = mark * lane

    def spread(d):
        for i, (j, _) in enumerate(batch_slots(d)):
            def put(k, carry, i=i, j=j):
                for base in (0, width):
                    slots[j, :, cols(k, base)] = lax.dot_general(
                        sel_buf[j], back[i * cap : (i + 1) * cap, cols(k, base)], contract0,
                        preferred_element_type=f32,
                    ).astype(bf16)
                return carry

            over_chunks(put)

    started = {}

    def begin(key, copies):
        started[key] = copies
        for c in copies:
            c.start()

    def got(key):
        for c in started[key]:
            c.wait_recv()

    def sent(key):
        for c in started[key]:
            c.wait_send()

    def finish(d):
        if d < half:
            sent(("ag", d + 1))
        for o in offsets(d):
            sent(("twin", o))
        spread(d)
        for o in offsets(d):
            begin(("part", o), partial_copies(o))

    begin(("ag", 1), gather_copies(1))
    begin(("twin", 0), twin_copies(0))
    for c in loads[3:]:
        c.wait()
    got(("twin", 0))
    compute(0)
    for s in range(1, half + 1):
        got(("ag", s))
        if s < half:
            begin(("ag", s + 1), gather_copies(s + 1))
        for o in offsets(s):
            begin(("twin", o), twin_copies(o))
        finish(s - 1)
        for o in offsets(s):
            got(("twin", o))
        compute(s)
    finish(half)

    def add_into(o, arrived, bases):
        def body(k, carry):
            for base, extra in zip((0, width), bases):
                total = slots[o, :, cols(k, base)].astype(f32) + sib[o, :, cols(k, base)].astype(f32)
                for side, step in extra:
                    total = total + ring[side, step, :, cols(k, base)].astype(f32)
                slots[o, :, cols(k, base)] = total.astype(bf16)
            return carry

        over_chunks(body)
        tile = gates[o] + sib_t[o]
        for side, step in arrived:
            tile = tile + ring_t[side, step]
        gates[o] = tile

    def weight_grads(which):
        out, rhs = ((og_ref, gpre), (ou_ref, upre), (od_ref, None))[which]

        def body(k, carry):
            c = pl.ds(pl.multiple_of(k * 256, 256), 256)
            if rhs is not None:
                out[c, :] = lax.dot_general(
                    rows[:, c], rhs[...], contract0, preferred_element_type=f32
                ).astype(bf16)
            else:
                c2 = pl.ds(pl.multiple_of(width + k * 256, 256), 256)
                out[:, c] = lax.dot_general(
                    hid[...], rows[:, c2], contract0, preferred_element_type=f32
                ).astype(bf16)
            return carry

        lax.fori_loop(0, width // 256, body, 0)

    for s in range(1, half + 1):
        o = half + 1 - s
        i = s - 1
        if s == 1:
            got(("part", o))
            add_into(o, [], ([], []))
            begin(("rs", s), [
                remote(slots.at[o, :, lo], ring.at[0, i, :, lo], rs_send.at[0, i], rs_recv.at[0, i], right),
                remote(slots.at[o, :, hi], ring.at[1, i, :, hi], rs_send.at[1, i], rs_recv.at[1, i], left),
                remote(gates.at[o], ring_t.at[0, i], rst_send.at[0, i], rst_recv.at[0, i], right),
            ])
        else:
            n = (-o) % chips
            got(("part", o))
            got(("part", n))
            got(("rs", s - 1))
            here = [[(0, i - 1)], [(1, i - 1)]]
            add_into(o, here[0], (here[0], here[0] if s > 2 else []))
            copies = [
                remote(slots.at[o], ring.at[0, i], rs_send.at[0, i], rs_recv.at[0, i], right),
                remote(gates.at[o], ring_t.at[0, i], rst_send.at[0, i], rst_recv.at[0, i], right),
                remote(slots.at[n], ring.at[1, i], rs_send.at[1, i], rs_recv.at[1, i], left),
                remote(gates.at[n], ring_t.at[1, i], rst_send.at[1, i], rst_recv.at[1, i], left),
            ]
            for c in copies[:2]:
                c.start()
            add_into(n, here[1] if s > 2 else [], (here[1] if s > 2 else [], here[1]))
            for c in copies[2:]:
                c.start()
            started[("rs", s)] = copies
        if s <= 3:
            weight_grads(s - 1)
    got(("part", 0))
    got(("rs", half))
    last = half - 1

    def final(k, carry):
        for out, base in ((eo_ref, 0), (gt_ref, width)):
            out[:, cols(k)] = (
                slots[0, :, cols(k, base)].astype(f32)
                + sib[0, :, cols(k, base)].astype(f32)
                + ring[0, last, :, cols(k, base)].astype(f32)
                + ring[1, last, :, cols(k, base)].astype(f32)
            ).astype(bf16)
        return carry

    over_chunks(final)
    gg_ref[...] = gates[0] + sib_t[0] + ring_t[0, last] + ring_t[1, last]
    for o in range(chips):
        sent(("part", o))
    for s in range(1, half + 1):
        sent(("rs", s))


def ring_layer(y_size, tokens, cotangent, route_ids, gate_probs, w_gate, w_up, w_down):
    owners = lax.axis_size("owner")
    chips = owners // 2
    half = chips // 2
    tok, width = tokens.shape
    routes = route_ids.shape[1]
    ffw = w_gate.shape[2]
    cap = -(-(2 * tok * routes // owners) // 16) * 16
    cap = min(cap, tok)
    bf16, f32 = jnp.bfloat16, jnp.float32
    route_t = jnp.pad(
        route_ids.reshape(owners, tok, routes).transpose(0, 2, 1),
        ((0, 0), (0, 8 - routes), (0, 0)), constant_values=-1,
    )
    prob_t = jnp.pad(gate_probs.T, ((0, 8 - routes), (0, 0)))
    vmem = pl.BlockSpec(memory_space=pltpu.VMEM)
    hbm = pl.BlockSpec(memory_space=pl.ANY)
    dma = pltpu.SemaphoreType.DMA
    total = owners * cap
    ring_sems = [dma((2, half))] * 4
    chip_sems = [dma((chips,))] * 4
    eo, gt, gg, og, ou, od = pl.pallas_call(
        functools.partial(ring_kernel, y_size, owners, cap),
        out_shape=(
            jax.ShapeDtypeStruct((tok, width), bf16),
            jax.ShapeDtypeStruct((tok, width), bf16),
            jax.ShapeDtypeStruct((8, tok), f32),
            jax.ShapeDtypeStruct((width, ffw), bf16),
            jax.ShapeDtypeStruct((width, ffw), bf16),
            jax.ShapeDtypeStruct((ffw, width), bf16),
        ),
        in_specs=[vmem, hbm, hbm, hbm, hbm, hbm, hbm],
        out_specs=(vmem,) * 6,
        scratch_shapes=[
            pltpu.VMEM((owners, tok, 2 * width), bf16),
            pltpu.VMEM((owners, 8, tok), f32),
            pltpu.VMEM((chips, tok, 2 * width), bf16),
            pltpu.VMEM((chips, 8, tok), f32),
            pltpu.VMEM((2, half, tok, 2 * width), bf16),
            pltpu.VMEM((2, half, 8, tok), f32),
            pltpu.VMEM((owners, 8, tok), f32),
            pltpu.VMEM((owners, cap, tok), bf16),
            pltpu.VMEM((total, 2 * width), bf16),
            pltpu.VMEM((4 * cap, width), bf16),
            pltpu.VMEM((4 * cap, 1), f32),
            pltpu.VMEM((4 * cap, 2 * width), bf16),
            pltpu.VMEM((total, ffw), bf16),
            pltpu.VMEM((total, ffw), bf16),
            pltpu.VMEM((total, ffw), bf16),
            pltpu.VMEM((width, ffw), bf16),
            pltpu.VMEM((width, ffw), bf16),
            pltpu.VMEM((ffw, width), bf16),
        ] + ring_sems + chip_sems + chip_sems + ring_sems + [dma((6,))],
        compiler_params=pltpu.CompilerParams(
            collective_id=0, has_side_effects=True, vmem_limit_bytes=62 * 2**20
        ),
        cost_estimate=pl.CostEstimate(
            flops=18 * total * width * ffw, bytes_accessed=16 * width * ffw, transcendentals=0
        ),
        name="ring_layer",
    )(route_t, prob_t, tokens, cotangent, w_gate[0], w_up[0], w_down[0])
    return eo, gt, gg[:routes].T, og[None], ou[None], od[None]


def solution(mesh):
    owners = mesh.shape["owner"]
    chips = owners // 2
    y_size = ring_width(mesh)

    def run(tokens, cotangent, route_ids, gate_probs, w_gate, w_up, w_down):
        block = tokens.shape[0] * tokens.shape[1] * 4
        fits = owners * 2 * block <= 36 * 2**20
        if not fits or owners % 2 or chips < 4 or chips % 2:
            return local(tokens, cotangent, route_ids, gate_probs, w_gate, w_up, w_down)
        return ring_layer(
            y_size, tokens, cotangent, route_ids, gate_probs, w_gate, w_up, w_down
        )

    placed = (
        P(("group", "owner"), None),
        P(("group", "owner"), None),
        P("group", None),
        P(("group", "owner"), None),
        P("owner", None, None),
        P("owner", None, None),
        P("owner", None, None),
    )
    return jax.shard_map(
        run,
        mesh=mesh,
        in_specs=placed,
        out_specs=(
            P(("group", "owner"), None),
            P(("group", "owner"), None),
            P(("group", "owner"), None),
            P(("group", "owner"), None, None),
            P(("group", "owner"), None, None),
            P(("group", "owner"), None, None),
        ),
        check_vma=False,
    )
```

profile of v0, /device:TPU:0, one launch (start us, length us, event | category | flops | bytes accessed | tf_op | source)
XLA Modules:
  0.0 207.0 jit_solution(15015856953017497522)
XLA Ops:
  0.6 1.3 pad.9.prob_ref
  1.9 1.4 pad.8.route_ref
  3.3 193.4 %ring_layer.1 = (bf16[128,2048]{1,0:T(8,128)(2,1)}, bf16[128,2048]{1,0:T(8,128)(2,1)}, f32[8,128]{1,0:T(8,128)}, bf16[2048,384]{1,0:T(8,128)(2,1)}, bf16[2048,38...) custom-call(s32[16,8,128]{2,1,0:T(8,128)} %pad.8.route_ref, f32[8,128]{1,0:T(8,128)} %pad.9.prob_ref, bf16[128,2048]{1,0:T(8,128)(2,1)} %tok_ref.1, ...), custom_call_target="tpu_custom_call" | custom-call | flops 10871635968 | bytes 12582912 | tf_op jit(solution)/shard_map/ring_layer/pallas_call | solution.py:492
  196.7 0.0 copy-start.2
  196.7 1.4 slice_bitcast_fusion
  198.1 1.9 copy.18
  200.0 1.9 copy.19
  201.9 0.0 copy-done.2
  201.9 0.0 copy-start.1
  201.9 1.1 copy.20
  203.0 0.8 copy-done.1
  203.9 0.0 copy-start
  203.9 1.1 copy.21
  205.0 0.8 copy-done
  205.8 1.1 copy.22
Async XLA Ops:
  196.7 5.2 %copy-start.2 = (bf16[2048,384]{1,0:T(8,128)(2,1)S(1)}, bf16[2048,384]{1,0:T(8,128)(2,1)}, u32[]{:S(2)}) copy-start(bf16[2048,384]{1,0:T(8,128)(2,1)} %get-tuple-element.15) | copy-start | bytes 4718596
  201.9 2.0 copy-start.1
  203.9 2.0 copy-start
where the time goes:
time: 207 us
  Pallas kernels  193 us (93%)
  local copies, waits for them, and re-layouts  12.9 us (6%)
    pallas_call x1, Pallas kernels, ring_layer(): pl.pallas_call(functools.partial(ring_kernel, y_size, owners, cap), out_s...  193 us
    unnamed x11, local copies, waits for them, and re-layouts  8.86 us

commit v1 on v0

--- a/solution.py
+++ b/solution.py
@@ -25,6 +25,15 @@
         + jnp.dot(grad_up_pre, up_w.T, preferred_element_type=jnp.float32)
     ).astype(jnp.bfloat16)
     return (expert_y, expert_dx, hidden, grad_gate_pre, grad_up_pre)
+
+
+def running_sum(flags):
+    count = flags.shape[0]
+    at = jnp.arange(count, dtype=jnp.int32)
+    lower = (at[:, None] >= at[None, :]).astype(jnp.bfloat16)
+    return jnp.dot(
+        lower, flags.astype(jnp.bfloat16), preferred_element_type=jnp.float32
+    ).astype(jnp.int32)
 
 
 def local(tokens, cotangent, route_ids, gate_probs, w_gate, w_up, w_down):
@@ -39,7 +48,7 @@
     id_table = route_ids.reshape(owner_count, assign_count)
     my_routes = lax.dynamic_index_in_dim(id_table, my_index, 0, keepdims=False)
     one_hot = (my_routes[:, None] == expert_ids[None, :]).astype(jnp.int32)
-    rank_within = jnp.sum((jnp.cumsum(one_hot, axis=0) - one_hot) * one_hot, axis=1)
+    rank_within = jnp.sum((running_sum(one_hot) - one_hot) * one_hot, axis=1)
     source_loads = jnp.sum((id_table == my_index).astype(jnp.int32), axis=1)
     scaled_cot = (gate_probs[:, :, None] * cotangent[:, None, :].astype(jnp.float32)).astype(
         jnp.bfloat16
@@ -63,7 +72,7 @@
     live_slot = (jnp.arange(slot_depth, dtype=jnp.int32)[None, :] < source_loads[:, None]).reshape(
         slot_total
     )
-    compact_pos = jnp.cumsum(live_slot.astype(jnp.int32)) - 1
+    compact_pos = running_sum(live_slot.astype(jnp.int32)[:, None])[:, 0] - 1
     live_total = jnp.sum(source_loads)
     compact_from = jnp.full((slot_total,), slot_total, jnp.int32)
     compact_from = compact_from.at[jnp.where(live_slot, compact_pos, slot_total)].set(
@@ -202,22 +211,27 @@
 
     lo, hi = pl.ds(0, width), pl.ds(width, width)
 
-    def gather_copies(s):
+    def gather_copies(s, part):
         a, b = (-(s - 1)) % chips, s - 1
         c, d = (-s) % chips, s
         i = s - 1
-        if s < half:
-            return [
-                remote(slots.at[a], slots.at[c], ag_send.at[0, i], ag_recv.at[0, i], right),
-                remote(slots.at[b], slots.at[d], ag_send.at[1, i], ag_recv.at[1, i], left),
-                remote(probs.at[a], probs.at[c], agt_send.at[0, i], agt_recv.at[0, i], right),
-                remote(probs.at[b], probs.at[d], agt_send.at[1, i], agt_recv.at[1, i], left),
-            ]
-        return [
-            remote(slots.at[a, :, lo], slots.at[half, :, lo], ag_send.at[0, i], ag_recv.at[0, i], right),
-            remote(slots.at[b, :, hi], slots.at[half, :, hi], ag_send.at[1, i], ag_recv.at[1, i], left),
-            remote(probs.at[a], probs.at[half], agt_send.at[0, i], agt_recv.at[0, i], right),
-        ]
+        span = (lo, hi)[part]
+        out = []
+        if s < half or part == 0:
+            out.append(remote(
+                slots.at[a, :, span], slots.at[c, :, span],
+                ag_send.at[0, i, part], ag_recv.at[0, i, part], right,
+            ))
+        if s < half or part == 1:
+            out.append(remote(
+                slots.at[b, :, span], slots.at[d, :, span],
+                ag_send.at[1, i, part], ag_recv.at[1, i, part], left,
+            ))
+        if part == 0:
+            out.append(remote(probs.at[a], probs.at[c], agt_send.at[0, i], agt_recv.at[0, i], right))
+            if s < half:
+                out.append(remote(probs.at[b], probs.at[d], agt_send.at[1, i], agt_recv.at[1, i], left))
+        return out
 
     def twin_copies(o):
         return [
@@ -356,23 +370,26 @@
 
     def finish(d):
         if d < half:
-            sent(("ag", d + 1))
+            sent(("ag", d + 1, 0))
+            sent(("ag", d + 1, 1))
         for o in offsets(d):
             sent(("twin", o))
         spread(d)
         for o in offsets(d):
             begin(("part", o), partial_copies(o))
 
-    begin(("ag", 1), gather_copies(1))
+    for part in (0, 1):
+        begin(("ag", 1, part), gather_copies(1, part))
     begin(("twin", 0), twin_copies(0))
     for c in loads[3:]:
         c.wait()
     got(("twin", 0))
     compute(0)
     for s in range(1, half + 1):
-        got(("ag", s))
-        if s < half:
-            begin(("ag", s + 1), gather_copies(s + 1))
+        for part in (0, 1):
+            got(("ag", s, part))
+            if s < half:
+                begin(("ag", s + 1, part), gather_copies(s + 1, part))
         for o in offsets(s):
             begin(("twin", o), twin_copies(o))
         finish(s - 1)
@@ -381,20 +398,42 @@
         compute(s)
     finish(half)
 
-    def add_into(o, arrived, bases):
+    def add_into(o, base, arrived):
         def body(k, carry):
-            for base, extra in zip((0, width), bases):
-                total = slots[o, :, cols(k, base)].astype(f32) + sib[o, :, cols(k, base)].astype(f32)
-                for side, step in extra:
-                    total = total + ring[side, step, :, cols(k, base)].astype(f32)
-                slots[o, :, cols(k, base)] = total.astype(bf16)
+            total = slots[o, :, cols(k, base)].astype(f32) + sib[o, :, cols(k, base)].astype(f32)
+            for side, step in arrived:
+                total = total + ring[side, step, :, cols(k, base)].astype(f32)
+            slots[o, :, cols(k, base)] = total.astype(bf16)
             return carry
 
         over_chunks(body)
+
+    def add_tile(o, arrived):
         tile = gates[o] + sib_t[o]
         for side, step in arrived:
             tile = tile + ring_t[side, step]
         gates[o] = tile
+
+    def send_sum(side, s, part):
+        o = half + 1 - s if side == 0 else (s - half - 1) % chips
+        i = s - 1
+        to = right if side == 0 else left
+        arrived = []
+        if ("rs", side, s - 1, part) in started:
+            got(("rs", side, s - 1, part))
+            arrived = [(side, s - 2)]
+        add_into(o, part * width, arrived)
+        span = (lo, hi)[part]
+        copies = [remote(
+            slots.at[o, :, span], ring.at[side, i, :, span],
+            rs_send.at[side, i, part], rs_recv.at[side, i, part], to,
+        )]
+        if (side == 0 or s > 1) and part == side:
+            add_tile(o, arrived if side == 0 or s > 2 else [])
+            copies.append(remote(
+                gates.at[o], ring_t.at[side, i], rst_send.at[side, i], rst_recv.at[side, i], to,
+            ))
+        begin(("rs", side, s, part), copies)
 
     def weight_grads(which):
         out, rhs = ((og_ref, gpre), (ou_ref, upre), (od_ref, None))[which]
@@ -414,40 +453,23 @@
 
         lax.fori_loop(0, width // 256, body, 0)
 
-    for s in range(1, half + 1):
-        o = half + 1 - s
-        i = s - 1
-        if s == 1:
+    got(("part", half))
+    send_sum(0, 1, 0)
+    send_sum(1, 1, 1)
+    for s in range(2, half + 1):
+        for o in offsets(half + 1 - s):
             got(("part", o))
-            add_into(o, [], ([], []))
-            begin(("rs", s), [
-                remote(slots.at[o, :, lo], ring.at[0, i, :, lo], rs_send.at[0, i], rs_recv.at[0, i], right),
-                remote(slots.at[o, :, hi], ring.at[1, i, :, hi], rs_send.at[1, i], rs_recv.at[1, i], left),
-                remote(gates.at[o], ring_t.at[0, i], rst_send.at[0, i], rst_recv.at[0, i], right),
-            ])
-        else:
-            n = (-o) % chips
-            got(("part", o))
-            got(("part", n))
-            got(("rs", s - 1))
-            here = [[(0, i - 1)], [(1, i - 1)]]
-            add_into(o, here[0], (here[0], here[0] if s > 2 else []))
-            copies = [
-                remote(slots.at[o], ring.at[0, i], rs_send.at[0, i], rs_recv.at[0, i], right),
-                remote(gates.at[o], ring_t.at[0, i], rst_send.at[0, i], rst_recv.at[0, i], right),
-                remote(slots.at[n], ring.at[1, i], rs_send.at[1, i], rs_recv.at[1, i], left),
-                remote(gates.at[n], ring_t.at[1, i], rst_send.at[1, i], rst_recv.at[1, i], left),
-            ]
-            for c in copies[:2]:
-                c.start()
-            add_into(n, here[1] if s > 2 else [], (here[1] if s > 2 else [], here[1]))
-            for c in copies[2:]:
-                c.start()
-            started[("rs", s)] = copies
-        if s <= 3:
-            weight_grads(s - 1)
+        send_sum(0, s, 1)
+        send_sum(1, s, 0)
+        if s <= 4:
+            weight_grads(s - 2)
+        send_sum(0, s, 0)
+        send_sum(1, s, 1)
+    for which in range(max(half - 1, 0), 3):
+        weight_grads(which)
     got(("part", 0))
-    got(("rs", half))
+    for side, part in ((0, 1), (1, 0), (0, 0), (1, 1)):
+        got(("rs", side, half, part))
     last = half - 1
 
     def final(k, carry):
@@ -464,8 +486,9 @@
     gg_ref[...] = gates[0] + sib_t[0] + ring_t[0, last] + ring_t[1, last]
     for o in range(chips):
         sent(("part", o))
-    for s in range(1, half + 1):
-        sent(("rs", s))
+    for key in list(started):
+        if key[0] == "rs":
+            sent(key)
 
 
 def ring_layer(y_size, tokens, cotangent, route_ids, gate_probs, w_gate, w_up, w_down):
@@ -487,7 +510,8 @@
     hbm = pl.BlockSpec(memory_space=pl.ANY)
     dma = pltpu.SemaphoreType.DMA
     total = owners * cap
-    ring_sems = [dma((2, half))] * 4
+    part_sems = [dma((2, half, 2))] * 2
+    ring_sems = part_sems + [dma((2, half))] * 2
     chip_sems = [dma((chips,))] * 4
     eo, gt, gg, og, ou, od = pl.pallas_call(
         functools.partial(ring_kernel, y_size, owners, cap),

time: 207 us -> 200 us (0.966)
  Pallas kernels: 193 us -> 186 us
    pallas_call x1, Pallas kernels: 193 us -> 186 us  [ring_layer(): pl.pallas_call(functools.partial(ring_kernel, y_size, owners, cap), out_s...]
where the time goes in v1:
time: 200 us; the launch traced here: 199 us
  Pallas kernels  186 us (93%)
  local copies, waits for them, and re-layouts  12.9 us (6%)
    pallas_call x1, Pallas kernels, ring_layer(): pl.pallas_call(functools.partial(ring_kernel, y_size, owners, cap), out_s...  186 us
    unnamed x11, local copies, waits for them, and re-layouts  8.86 us

profile of v1, /device:TPU:0, one launch (start us, length us, event | category | flops | bytes accessed | tf_op | source)
XLA Modules:
  0.0 199.3 jit_solution(5018932640574366035)
XLA Ops:
  0.6 1.3 pad.9.prob_ref
  1.9 1.4 pad.8.route_ref
  3.3 185.7 %ring_layer.1 = (bf16[128,2048]{1,0:T(8,128)(2,1)}, bf16[128,2048]{1,0:T(8,128)(2,1)}, f32[8,128]{1,0:T(8,128)}, bf16[2048,384]{1,0:T(8,128)(2,1)}, bf16[2048,38...) custom-call(s32[16,8,128]{2,1,0:T(8,128)} %pad.8.route_ref, f32[8,128]{1,0:T(8,128)} %pad.9.prob_ref, bf16[128,2048]{1,0:T(8,128)(2,1)} %tok_ref.1, ...), custom_call_target="tpu_custom_call" | custom-call | flops 10871635968 | bytes 12582912 | tf_op jit(solution)/shard_map/ring_layer/pallas_call | solution.py:516
  189.0 0.0 copy-start.2
  189.1 1.4 slice_bitcast_fusion
  190.4 1.9 copy.18
  192.3 1.9 copy.19
  194.2 0.0 copy-done.2
  194.2 0.0 copy-start.1
  194.2 1.1 copy.20
  195.3 0.8 copy-done.1
  196.2 0.0 copy-start
  196.2 1.1 copy.21
  197.3 0.8 copy-done
  198.2 1.1 copy.22
Async XLA Ops:
  189.0 5.2 %copy-start.2 = (bf16[2048,384]{1,0:T(8,128)(2,1)S(1)}, bf16[2048,384]{1,0:T(8,128)(2,1)}, u32[]{:S(2)}) copy-start(bf16[2048,384]{1,0:T(8,128)(2,1)} %get-tuple-element.15) | copy-start | bytes 4718596
  194.2 2.0 copy-start.1
  196.2 2.0 copy-start
